TPU v7x, 32 devices: a whole 2x2x4 slice. The times are simulated.
32 devices in a mesh: group: 2 (over y), section: 4 (over z), dp: 4 (over x, core).
Axes of the slice: x: 2, y: 2, z: 4, core: 2. Of those that a mesh axis runs over, the one named last changes fastest.
Arguments:
- tokens: bfloat16 [4, 8, 32, 1600], P(None, ('group', 'dp')), parts along dimension 1, may hold values from -6 to 6
- pixel_index: int32 [4, 8, 384], P(None, ('group', 'dp')), parts along dimension 1, may hold values from 0 to 6271
- point_mask: int32 [4, 8, 384], P(None, ('group', 'dp')), parts along dimension 1, may hold values from 0 to 1, as said below
- point_depth: float32 [4, 8, 384], P(None, ('group', 'dp')), parts along dimension 1, may hold values from -6 to 6
- hook_section: int32 [4], replicated, may hold values from 0 to 2, as said below
- w_query: bfloat16 [4, 1600, 832], P('section')
- w_key: bfloat16 [4, 1600, 832], P('section')
- w_value: bfloat16 [4, 1600, 832], P('section'), may hold values from -0.15625 to 0.15625
- w_output: bfloat16 [4, 832, 1600], P('section'), may hold values from -0.21875 to 0.21875
- reassemble: bfloat16 [5, 1600, 128], P(None, None, ('section', 'dp')), may hold values from -0.15625 to 0.15625
- merging: bfloat16 [4, 128, 128], P(None, None, ('section', 'dp')), may hold values from -0.5 to 0.5
- predict: bfloat16 [128, 196], P(('section', 'dp')), may hold values from -0.5 to 0.5
Outputs:
- grad_query: bfloat16 [8, 1600, 832], P(('group', 'section'), 'dp'), parts along dimension 0
- grad_key: bfloat16 [8, 1600, 832], P(('group', 'section'), 'dp'), parts along dimension 0
- grad_value: bfloat16 [8, 1600, 832], P(('group', 'section'), 'dp'), parts along dimension 0
- grad_output: bfloat16 [8, 832, 1600], P(('group', 'section'), 'dp'), parts along dimension 0
- grad_reassemble: float32 [10, 1600, 128], P('group', None, ('section', 'dp')), parts along dimension 0
- grad_merging: float32 [8, 128, 128], P('group', None, ('section', 'dp')), parts along dimension 0
- grad_predict: float32 [256, 196], P(('group', 'section', 'dp')), parts along dimension 0
There are 2 independent parts, one for each index of `group`. A program takes and returns all parts, laid end to end along the dimension named above; an argument that names none is the same for every part. Nothing has to cross between parts.
Inputs may be any that keep to these rules, and one draw needn't show every extreme that they name: `point_mask`: in each image the valid points come first, and at least 48 of them are valid. `hook_section`: Sorted; the last entry is 2.
All inputs are finite; a program needn't handle non-finite values.
Results may differ from a plain program's by a relative error of at most 0.03.
Values may be sent and summed in bfloat16 or wider, within the bound.
A program may use at most 128 MiB of HBM per device.

v0:
```python
import math
import jax
import jax.numpy as jnp
from jax import lax
from jax.sharding import PartitionSpec as P

HEADS = 13
NHOOK = 4
EPS = 1e-06


def passed_along(block, axis, distance):
    devices = range(lax.axis_size(axis))
    route = [(i - distance, i) for i in devices if i - distance in devices]
    return lax.ppermute(block, axis, route)


def broadcast(value, axis, source):
    kept = jnp.where(lax.axis_index(axis) == source, value, 0).astype(value.dtype)
    return lax.psum(kept, axis)


def as_sent(x):
    return jax.tree.map(lambda a: a.astype(jnp.bfloat16) if a.dtype == jnp.float32 else a, x)


def rms_normed(stream):
    widened = stream.astype(jnp.float32)
    inv_root = lax.rsqrt(jnp.mean(widened * widened, axis=-1, keepdims=True) + EPS)
    return (widened * inv_root).astype(jnp.bfloat16)


def attend(query_rows, key_rows, value_rows):
    image_count, token_count, inner_width = query_rows.shape
    head_width = inner_width // HEADS
    shape_heads = (image_count, token_count, HEADS, head_width)
    query_heads = query_rows.astype(jnp.float32).reshape(shape_heads)
    key_heads = key_rows.astype(jnp.float32).reshape(shape_heads)
    value_heads = value_rows.astype(jnp.float32).reshape(shape_heads)
    scores = jnp.einsum("bqhe,bkhe->bhqk", query_heads, key_heads) / math.sqrt(head_width)
    probabilities = jax.nn.softmax(scores, axis=-1).astype(jnp.bfloat16)
    mixed_heads = jnp.einsum("bhqk,bkhe->bqhe", probabilities.astype(jnp.float32), value_heads)
    return mixed_heads.reshape(image_count, token_count, inner_width).astype(jnp.bfloat16)


def attention_layer(stream, layer_query, layer_key, layer_value, layer_output, nudges):
    image_count, token_count, model_width = stream.shape
    normed = rms_normed(stream).reshape(image_count * token_count, model_width)
    query_rows = (
        jnp.dot(normed, layer_query, preferred_element_type=jnp.float32).astype(jnp.bfloat16)
        + nudges[0]
    )
    key_rows = (
        jnp.dot(normed, layer_key, preferred_element_type=jnp.float32).astype(jnp.bfloat16)
        + nudges[1]
    )
    value_rows = (
        jnp.dot(normed, layer_value, preferred_element_type=jnp.float32).astype(jnp.bfloat16)
        + nudges[2]
    )
    inner_width = layer_query.shape[1]
    mixed = attend(
        query_rows.reshape(image_count, token_count, inner_width),
        key_rows.reshape(image_count, token_count, inner_width),
        value_rows.reshape(image_count, token_count, inner_width),
    )
    mixed_rows = mixed.reshape(image_count * token_count, inner_width)
    update = jnp.dot(mixed_rows, layer_output, preferred_element_type=jnp.float32)
    update = update.reshape(image_count, token_count, model_width)
    output_rows = stream.astype(jnp.float32) + update
    return (output_rows, (normed, mixed_rows))


def reassemble_map(features, weight):
    flat_rows = features.reshape(-1, features.shape[-1]).astype(jnp.bfloat16)
    return jnp.dot(flat_rows, weight, preferred_element_type=jnp.float32).astype(jnp.bfloat16)


def head_rest(projected, top_projected, merging, predict, pixel_index, point_mask, point_depth):
    merged = top_projected.astype(jnp.float32)
    for hook_slot in range(len(projected) - 1, -1, -1):
        activated = jax.nn.silu(merged).astype(jnp.bfloat16)
        merged = projected[hook_slot].astype(jnp.float32) + jnp.dot(
            activated, merging[hook_slot], preferred_element_type=jnp.float32
        )
    activated = jax.nn.silu(merged).astype(jnp.bfloat16)
    depth_rows = jnp.dot(activated, predict, preferred_element_type=jnp.float32)
    depth_map = depth_rows.reshape(pixel_index.shape[0], pixel_index.shape[1], -1)
    picked = jnp.take_along_axis(depth_map, pixel_index, axis=2)
    valid_mask = point_mask.astype(jnp.float32)
    valid_count = jnp.sum(valid_mask, axis=2)
    misfit = (picked - point_depth) * valid_mask
    return jnp.sum(jnp.sum(misfit * misfit, axis=2) / valid_count)


def keep_rows(stream):
    return stream


def put_slot(store_array, item_rows, micro_slot, active):
    updated = lax.dynamic_update_index_in_dim(store_array, item_rows, micro_slot, 0)
    return jnp.where(active, updated, store_array)


def contract(left_rows, right_rows):
    return jnp.einsum("mrd,mrh->dh", left_rows, right_rows, preferred_element_type=jnp.float32)


def on_device(
    tokens,
    pixel_index,
    point_mask,
    point_depth,
    hook_section,
    w_query,
    w_key,
    w_value,
    w_output,
    reassemble,
    merging,
    predict,
):
    section_index = lax.axis_index("section")
    section_count = lax.axis_size("section")
    last_section = section_count - 1
    is_last = section_index == last_section
    micro_count = tokens.shape[0]
    token_rows = tokens.shape[1] * tokens.shape[2]
    model_width = tokens.shape[3]
    inner_width = w_query.shape[2]
    layer_query = w_query[0]
    layer_key = w_key[0]
    layer_value = w_value[0]
    layer_output = w_output[0]
    full_reassemble, full_merging, full_predict = (
        lax.all_gather(reassemble, ("section", "dp"), axis=2, tiled=True),
        lax.all_gather(merging, ("section", "dp"), axis=2, tiled=True),
        lax.all_gather(predict, ("section", "dp"), axis=0, tiled=True),
    )
    zero_nudges = jnp.zeros((3, token_rows, inner_width), jnp.bfloat16)
    zero_rows = jnp.zeros(tokens.shape[1:], jnp.float32)
    empty_store = jnp.zeros(tokens.shape, jnp.float32)

    def run_layer(stream):
        return attention_layer(
            stream, layer_query, layer_key, layer_value, layer_output, zero_nudges
        )[0]

    def forward_step(time_step, carried):
        incoming, inputs_store, outputs_store = carried
        micro_index = time_step - section_index
        active = jnp.logical_and(micro_index >= 0, micro_index < micro_count)
        micro_slot = jnp.clip(micro_index, 0, micro_count - 1)
        fresh_rows = lax.dynamic_index_in_dim(tokens, micro_slot, 0, keepdims=False).astype(
            jnp.float32
        )
        source = jnp.where(section_index == 0, fresh_rows, incoming)
        result = lax.cond(active, run_layer, keep_rows, source)
        inputs_store = put_slot(inputs_store, source, micro_slot, active)
        outputs_store = put_slot(outputs_store, result, micro_slot, active)
        incoming = passed_along(result, "section", 1)
        return (incoming, inputs_store, outputs_store)

    unused, inputs_store, outputs_store = lax.fori_loop(
        0, micro_count + section_count - 1, forward_step, (zero_rows, empty_store, empty_store)
    )
    hook_sum = jnp.zeros(tokens.shape, jnp.float32)
    received = []
    for hook_slot in range(NHOOK):
        local_piece = reassemble_map(outputs_store, full_reassemble[hook_slot])
        received.append(broadcast(local_piece, "section", hook_section[hook_slot]))
    projected_in = tuple(received)

    def head_grads(head_items):

        def loss_terms(projected, top_feature, reassemble_last, head_merging, head_predict):
            top_projected = reassemble_map(top_feature, reassemble_last)
            return head_rest(
                projected,
                top_projected,
                head_merging,
                head_predict,
                pixel_index,
                point_mask,
                point_depth,
            )

        loss_value, pullback = jax.vjp(
            loss_terms,
            head_items[0],
            head_items[1],
            full_reassemble[NHOOK],
            full_merging,
            full_predict,
        )
        return pullback(jnp.ones((), jnp.float32))

    def no_grads(head_items):
        return (
            tuple((jnp.zeros_like(array_item) for array_item in head_items[0])),
            jnp.zeros_like(head_items[1]),
            jnp.zeros_like(full_reassemble[NHOOK]),
            jnp.zeros_like(full_merging),
            jnp.zeros_like(full_predict),
        )

    projected_grads, last_grad, reassemble_last_grad, grad_merging, grad_predict = lax.cond(
        is_last, head_grads, no_grads, (projected_in, outputs_store)
    )
    projected_cotangents = broadcast(jnp.stack(projected_grads), "section", last_section)
    weight_grads = []
    for hook_slot in range(NHOOK):
        unused_rows, pullback = jax.vjp(reassemble_map, outputs_store, full_reassemble[hook_slot])
        feature_grad, weight_grad = pullback(projected_cotangents[hook_slot])
        is_owner = hook_section[hook_slot] == section_index
        hook_sum = hook_sum + jnp.where(is_owner, feature_grad, 0.0)
        weight_grads.append(jnp.where(is_owner, weight_grad, jnp.zeros_like(weight_grad)))
    weight_grads.append(reassemble_last_grad)
    grad_reassemble = jnp.stack(weight_grads)
    hook_grad = hook_sum

    def backward_one(stream, cotangent):

        def local_layer(entry_rows, nudges):
            return attention_layer(
                entry_rows, layer_query, layer_key, layer_value, layer_output, nudges
            )

        unused_rows, pullback, saved = jax.vjp(local_layer, stream, zero_nudges, has_aux=True)
        entry_grad, nudge_grad = pullback(cotangent)
        return (entry_grad, nudge_grad, saved[0], saved[1])

    def skip_one(stream, cotangent):
        return (
            jnp.zeros_like(stream),
            zero_nudges,
            jnp.zeros((token_rows, model_width), jnp.bfloat16),
            jnp.zeros((token_rows, inner_width), jnp.bfloat16),
        )

    def backward_step(time_step, carried):
        incoming, nudge_store, normed_store, mixed_store, cotangent_store = carried
        micro_index = time_step - (last_section - section_index)
        active = jnp.logical_and(micro_index >= 0, micro_index < micro_count)
        micro_slot = jnp.clip(micro_index, 0, micro_count - 1)
        upstream = jnp.where(
            is_last, lax.dynamic_index_in_dim(last_grad, micro_slot, 0, keepdims=False), incoming
        )
        cotangent = upstream + lax.dynamic_index_in_dim(hook_grad, micro_slot, 0, keepdims=False)
        stream = lax.dynamic_index_in_dim(inputs_store, micro_slot, 0, keepdims=False)
        entry_grad, nudge_grad, normed, mixed_rows = lax.cond(
            active, backward_one, skip_one, stream, cotangent
        )
        nudge_store = put_slot(nudge_store, nudge_grad, micro_slot, active)
        normed_store = put_slot(normed_store, normed, micro_slot, active)
        mixed_store = put_slot(mixed_store, mixed_rows, micro_slot, active)
        cotangent_store = put_slot(cotangent_store, cotangent, micro_slot, active)
        incoming = jax.tree.map(
            lambda part, own: part.astype(own.dtype),
            passed_along(as_sent(entry_grad), "section", -1),
            entry_grad,
        )
        return (incoming, nudge_store, normed_store, mixed_store, cotangent_store)

    start_state = (
        zero_rows,
        jnp.zeros((micro_count, 3, token_rows, inner_width), jnp.bfloat16),
        jnp.zeros((micro_count, token_rows, model_width), jnp.bfloat16),
        jnp.zeros((micro_count, token_rows, inner_width), jnp.bfloat16),
        empty_store,
    )
    unused, nudge_store, normed_store, mixed_store, cotangent_store = lax.fori_loop(
        0, micro_count + section_count - 1, backward_step, start_state
    )
    grad_query = contract(normed_store, nudge_store[:, 0])
    grad_key = contract(normed_store, nudge_store[:, 1])
    grad_value = contract(normed_store, nudge_store[:, 2])
    mixed_all = mixed_store.reshape(micro_count * token_rows, inner_width)
    update_grad = cotangent_store.reshape(micro_count * token_rows, model_width)

    def output_map(weight):
        return jnp.dot(mixed_all, weight, preferred_element_type=jnp.float32)

    unused_update, output_pullback = jax.vjp(output_map, layer_output)
    grad_output = output_pullback(update_grad)[0].astype(jnp.float32)
    summed_query, summed_key, summed_value, summed_output = (
        lax.psum_scatter(
            grad_query[None].astype(jnp.bfloat16), "dp", scatter_dimension=1, tiled=True
        ).astype(jnp.float32),
        lax.psum_scatter(
            grad_key[None].astype(jnp.bfloat16), "dp", scatter_dimension=1, tiled=True
        ).astype(jnp.float32),
        lax.psum_scatter(
            grad_value[None].astype(jnp.bfloat16), "dp", scatter_dimension=1, tiled=True
        ).astype(jnp.float32),
        lax.psum_scatter(
            grad_output[None].astype(jnp.bfloat16), "dp", scatter_dimension=1, tiled=True
        ).astype(jnp.float32),
    )
    head_reassemble, head_merging, head_predict = (
        lax.psum_scatter(
            grad_reassemble.astype(jnp.float32), ("section", "dp"), scatter_dimension=2, tiled=True
        ),
        lax.psum_scatter(
            grad_merging.astype(jnp.float32), ("section", "dp"), scatter_dimension=2, tiled=True
        ),
        lax.psum_scatter(
            grad_predict.astype(jnp.float32), ("section", "dp"), scatter_dimension=0, tiled=True
        ),
    )
    return (
        summed_query.astype(jnp.bfloat16),
        summed_key.astype(jnp.bfloat16),
        summed_value.astype(jnp.bfloat16),
        summed_output.astype(jnp.bfloat16),
        head_reassemble,
        head_merging,
        head_predict,
    )


def solution(mesh):
    placed = (
        P(None, ("group", "dp"), None, None),
        P(None, ("group", "dp"), None),
        P(None, ("group", "dp"), None),
        P(None, ("group", "dp"), None),
        P(),
        P("section", None, None),
        P("section", None, None),
        P("section", None, None),
        P("section", None, None),
        P(None, None, ("section", "dp")),
        P(None, None, ("section", "dp")),
        P(("section", "dp"), None),
    )
    return jax.shard_map(
        on_device,
        mesh=mesh,
        in_specs=placed,
        out_specs=(
            P(("group", "section"), "dp", None),
            P(("group", "section"), "dp", None),
            P(("group", "section"), "dp", None),
            P(("group", "section"), "dp", None),
            P("group", None, ("section", "dp")),
            P("group", None, ("section", "dp")),
            P(("group", "section", "dp"), None),
        ),
        check_vma=False,
    )
```

profile of v0, /device:TPU:0, one launch (start us, length us, event | category | flops | bytes accessed | tf_op | source)
XLA Modules:
  0.0 981.0 jit_solution(7728629565180497052)
XLA Ops:
  18.8 5.3 copy.216
  24.1 5.3 copy.214
  30.4 131.4 %while.42 = (s32[]{:T(128)}, f32[1,32,1600]{2,1,0:T(8,128)S(1)}, f32[4,1,32,1600]{3,2,1,0:T(8,128)}, bf16[4,1,32,1600]{3,2,1,0:T(8,128)(2,1)}, s32[]{:T(128)}, /...) while((s32[]{:T(128)}, f32[1,32,1600]{2,1,0:T(8,128)S(1)}, ...), condition=%wide.region_6.7_spmd, body=%wide.region_0.6_spmd.sunk | while | flops 344828992 | bytes 25776712 | solution.py:164
  32.1 10.4 %conditional.7 = (f32[1,32,1600]{2,1,0:T(8,128)S(1)}) conditional(s32[]{:T(128)} %convert_element_type.778, f32[1,32,1600]{2,1,0:T(8,128)S(1)} %get-tuple-element.1149, (f32[1,32,1600]{2,1,0:T(8,128)S(1)}, bf16[1600,832]{1,0:T(8,128)(2,1)}, bf16[1600,832]{1,0:T(8,128)(2,1)S(1)}, bf16[1600,832]{1,0:T(8,128)(2,1)}, bf16[832,1600]{1,0:T(8,128)(2,1)}) %tuple.167), branch_computations={%region_1.1_spmd, %region_2.5_spmd} | conditional | flops 344624192 | bytes 23596836 | solution.py:158
  45.4 7.6 collective-permute-done
  54.7 10.4 %conditional.7 = (f32[1,32,1600]{2,1,0:T(8,128)S(1)}) conditional(s32[]{:T(128)} %convert_element_type.778, f32[1,32,1600]{2,1,0:T(8,128)S(1)} %get-tuple-element.1149, (f32[1,32,1600]{2,1,0:T(8,128)S(1)}, bf16[1600,832]{1,0:T(8,128)(2,1)}, bf16[1600,832]{1,0:T(8,128)(2,1)S(1)}, bf16[1600,832]{1,0:T(8,128)(2,1)}, bf16[832,1600]{1,0:T(8,128)(2,1)}) %tuple.167), branch_computations={%region_1.1_spmd, %region_2.5_spmd} | conditional | flops 344624192 | bytes 23596836 | solution.py:158
  76.0 10.4 %conditional.7 = (f32[1,32,1600]{2,1,0:T(8,128)S(1)}) conditional(s32[]{:T(128)} %convert_element_type.778, f32[1,32,1600]{2,1,0:T(8,128)S(1)} %get-tuple-element.1149, (f32[1,32,1600]{2,1,0:T(8,128)S(1)}, bf16[1600,832]{1,0:T(8,128)(2,1)}, bf16[1600,832]{1,0:T(8,128)(2,1)S(1)}, bf16[1600,832]{1,0:T(8,128)(2,1)}, bf16[832,1600]{1,0:T(8,128)(2,1)}) %tuple.167), branch_computations={%region_1.1_spmd, %region_2.5_spmd} | conditional | flops 344624192 | bytes 23596836 | solution.py:158
  96.4 10.4 %conditional.7 = (f32[1,32,1600]{2,1,0:T(8,128)S(1)}) conditional(s32[]{:T(128)} %convert_element_type.778, f32[1,32,1600]{2,1,0:T(8,128)S(1)} %get-tuple-element.1149, (f32[1,32,1600]{2,1,0:T(8,128)S(1)}, bf16[1600,832]{1,0:T(8,128)(2,1)}, bf16[1600,832]{1,0:T(8,128)(2,1)S(1)}, bf16[1600,832]{1,0:T(8,128)(2,1)}, bf16[832,1600]{1,0:T(8,128)(2,1)}) %tuple.167), branch_computations={%region_1.1_spmd, %region_2.5_spmd} | conditional | flops 344624192 | bytes 23596836 | solution.py:158
  116.2 14.8 %collective-permute-start = (f32[1,32,1600]{2,1,0:T(8,128)S(1)}, f32[1,32,1600]{2,1,0:T(8,128)S(1)}, u32[]{:S(2)}, u32[]{:S(2)}) collective-permute-start(f32[1,32,1600]{2,1,0:T(8,128)S(1)} %get-tuple-element.1302), channel_id=1, source_target_pairs={{0,4},{4,8},{8,12},{1,5},{5,9},{9,13},{2,6},{6,10},{10,14},{3,7},{... | collective-permute-start | bytes 614408 | tf_op jit(solution)/shard_map/while/body/eval_jaxpr/ppermute | solution.py:15
  145.5 12.9 %collective-permute-start = (f32[1,32,1600]{2,1,0:T(8,128)S(1)}, f32[1,32,1600]{2,1,0:T(8,128)S(1)}, u32[]{:S(2)}, u32[]{:S(2)}) collective-permute-start(f32[1,32,1600]{2,1,0:T(8,128)S(1)} %get-tuple-element.1302), channel_id=1, source_target_pairs={{0,4},{4,8},{8,12},{1,5},{5,9},{9,13},{2,6},{6,10},{10,14},{3,7},{... | collective-permute-start | bytes 614408 | tf_op jit(solution)/shard_map/while/body/eval_jaxpr/ppermute | solution.py:15
  170.1 31.5 %all_gather.11 = bf16[128,196]{1,0:T(8,128)(2,1)S(1)} all-gather(bf16[8,196]{1,0:T(8,128)(2,1)S(1)} %copy-done.20), channel_id=1, replica_groups=mesh['group'=2,'section'=4,'dp'=4] {'section','dp'}, dimensions={0}, use_global_device_ids=true | all-gather | bytes 53312 | tf_op jit(solution)/shard_map/all_gather | solution.py:138
  201.6 17.9 %all_gather.10 = bf16[4,128,128]{1,0,2:T(4,128)(2,1)S(1)} all-gather(bf16[4,128,8]{1,0,2:T(4,128)(2,1)S(1)} %copy.217), channel_id=1, replica_groups=mesh['group'=2,'section'=4,'dp'=4] {'section','dp'}, dimensions={2}, use_global_device_ids=true | all-gather | bytes 139264 | tf_op jit(solution)/shard_map/all_gather | solution.py:137
  219.5 4.9 conditional.3
  228.7 75.9 %all-reduce.11.cloned.1.call-done = bf16[4,128,128]{2,1,0:T(8,128)(2,1)} async-done(((bf16[4,128,128]{2,1,0:T(8,128)(2,1)}), bf16[4,128,128]{2,1,0:T(8,128)(2,1)}) %all-reduce.11.cloned.1.call-update) | async-done | bytes 131088 | tf_op jit(solution)/shard_map/psum | solution.py:20
  315.7 278.6 %while.43 = (s32[]{:T(128)}, f32[1,32,1600]{2,1,0:T(8,128)S(1)}, bf16[4,3,32,832]{3,2,0,1:T(8,128)(2,1)}, bf16[4,32,1600]{2,1,0:T(8,128)(2,1)}, bf16[4,32,832]{2...) while((s32[]{:T(128)}, f32[1,32,1600]{2,1,0:T(8,128)S(1)}, ...), condition=%wide.region_24.25_spmd.clone, body=%wide.region_16.24_spmd.clone.sunk | while | flops 608857152 | bytes 61259056 | solution.py:272
  344.9 87.1 %collective-permute-done.1 = bf16[1,32,1600]{2,1,0:T(8,128)(2,1)S(1)} collective-permute-done((bf16[1,32,1600]{2,1,0:T(8,128)(2,1)}, bf16[1,32,1600]{2,1,0:T(8,128)(2,1)S(1)}, u32[]{:S(2)}, u32[]{:S(2)}) %collective-permute-start.1) | collective-permute-done | bytes 102432 | tf_op jit(solution)/shard_map/while/body/eval_jaxpr/ppermute | solution.py:15
  433.8 31.3 %conditional.8 = (bf16[1,32,1600]{2,1,0:T(8,128)(2,1)}, bf16[1,3,32,832]{3,2,1,0:T(8,128)(2,1)S(1)}, bf16[1,32,1600]{2,1,0:T(8,128)(2,1)}, bf16[1,32,832]{2,1,0:T(8,128)(2,1)S(1)}) conditional(s32[]{:T(128)} %convert_element_type.779, () %tuple.170, (f32[1,32,1600]{2,1,0:T(8,128)S(1)}, bf16[832,1600]{1,0:T(8,128)(2,1)}, ...), branch_computations={%region_17.17_spmd, %region_18.23_spmd} | conditional | flops 608443456 | bytes 57541052 | solution.py:251
  474.6 31.3 %conditional.8 = (bf16[1,32,1600]{2,1,0:T(8,128)(2,1)}, bf16[1,3,32,832]{3,2,1,0:T(8,128)(2,1)S(1)}, bf16[1,32,1600]{2,1,0:T(8,128)(2,1)}, bf16[1,32,832]{2,1,0:T(8,128)(2,1)S(1)}) conditional(s32[]{:T(128)} %convert_element_type.779, () %tuple.170, (f32[1,32,1600]{2,1,0:T(8,128)S(1)}, bf16[832,1600]{1,0:T(8,128)(2,1)}, ...), branch_computations={%region_17.17_spmd, %region_18.23_spmd} | conditional | flops 608443456 | bytes 57541052 | solution.py:251
  515.3 31.3 %conditional.8 = (bf16[1,32,1600]{2,1,0:T(8,128)(2,1)}, bf16[1,3,32,832]{3,2,1,0:T(8,128)(2,1)S(1)}, bf16[1,32,1600]{2,1,0:T(8,128)(2,1)}, bf16[1,32,832]{2,1,0:T(8,128)(2,1)S(1)}) conditional(s32[]{:T(128)} %convert_element_type.779, () %tuple.170, (f32[1,32,1600]{2,1,0:T(8,128)S(1)}, bf16[832,1600]{1,0:T(8,128)(2,1)}, ...), branch_computations={%region_17.17_spmd, %region_18.23_spmd} | conditional | flops 608443456 | bytes 57541052 | solution.py:251
  556.0 31.3 %conditional.8 = (bf16[1,32,1600]{2,1,0:T(8,128)(2,1)}, bf16[1,3,32,832]{3,2,1,0:T(8,128)(2,1)S(1)}, bf16[1,32,1600]{2,1,0:T(8,128)(2,1)}, bf16[1,32,832]{2,1,0:T(8,128)(2,1)S(1)}) conditional(s32[]{:T(128)} %convert_element_type.779, () %tuple.170, (f32[1,32,1600]{2,1,0:T(8,128)S(1)}, bf16[832,1600]{1,0:T(8,128)(2,1)}, ...), branch_computations={%region_17.17_spmd, %region_18.23_spmd} | conditional | flops 608443456 | bytes 57541052 | solution.py:251
  596.3 12.4 %copy.242 = bf16[1,1600,832]{2,0,1:T(2,128)(2,1)} copy(bf16[1,1600,832]{1,2,0:T(8,128)(2,1)S(1)} %fusion.92) | data formatting | bytes 5324800
  608.8 4.7 copy.332
  617.2 14.5 %copy.244 = bf16[1,1600,832]{2,0,1:T(2,128)(2,1)} copy(bf16[1,1600,832]{1,2,0:T(8,128)(2,1)} %fusion.93) | data formatting | bytes 5324800
  631.7 4.6 copy.331
  639.1 14.4 %copy.240 = bf16[1,1600,832]{2,0,1:T(2,128)(2,1)} copy(bf16[1,1600,832]{1,2,0:T(8,128)(2,1)} %fusion.91) | data formatting | bytes 5324800
  664.7 4.8 copy.229
  679.4 8.6 reduce-scatter.26.cloned.1.call-done
  690.7 35.9 %reduce-scatter.22.cloned.1.call-done = bf16[400,832]{1,0:T(8,128)(2,1)} async-done(((bf16[1600,832]{1,0:T(8,128)(2,1)}), bf16[400,832]{1,0:T(8,128)(2,1)}) %reduce-scatter.22.cloned.1.call-update) | async-done | bytes 665616
  729.4 90.1 %reduce-scatter.18.cloned.1.call-done = f32[5,1600,8]{1,0,2:T(8,128)} async-done(((f32[5,1600,128]{1,0,2:T(8,128)}), f32[5,1600,8]{1,0,2:T(8,128)}) %reduce-scatter.18.cloned.1.call-update) | async-done | bytes 256016 | tf_op jit(solution)/shard_map/reduce_scatter | solution.py:301
  821.3 56.8 %reduce-scatter.28.cloned.1.call-done = f32[8,196]{1,0:T(8,128)} async-done(((f32[128,196]{1,0:T(8,128)}), f32[8,196]{1,0:T(8,128)}) %reduce-scatter.28.cloned.1.call-update) | async-done | bytes 6288
  878.1 58.5 %reduce-scatter.20.cloned.1.call-done = f32[4,128,8]{1,2,0:T(8,128)} async-done(((f32[4,128,128]{1,2,0:T(8,128)}), f32[4,128,8]{1,2,0:T(8,128)}) %reduce-scatter.20.cloned.1.call-update) | async-done | bytes 16400 | tf_op jit(solution)/shard_map/reduce_scatter | solution.py:304
  936.6 37.6 %reduce-scatter.16.cloned.1.call-done = bf16[1,208,1600]{2,1,0:T(8,128)(2,1)} async-done(((bf16[1,832,1600]{2,1,0:T(8,128)(2,1)}), bf16[1,208,1600]{2,1,0:T(8,128)(2,1)}) %reduce-scatter.16.cloned.1.call-update) | async-done | bytes 665616 | tf_op jit(solution)/shard_map/reduce_scatter | solution.py:296
  (456 shorter events, 362.8 us)
Async XLA Ops:
  7.2 154.6 %all-gather.2.cloned.1.call-start = ((), (), s32[]{:S(2)}) async-start(), calls=%async_computation.7 | async-start | bytes 2263040 | tf_op jit(solution)/shard_map/all_gather | solution.py:136
  7.9 211.6 %all-reduce.13.cloned.1.call-start = ((), (), s32[]{:S(2)}) async-start(), calls=%async_computation.16 | async-start | bytes 262144 | tf_op jit(solution)/shard_map/psum | solution.py:20
  42.5 10.5 %collective-permute-start = (f32[1,32,1600]{2,1,0:T(8,128)S(1)}, f32[1,32,1600]{2,1,0:T(8,128)S(1)}, u32[]{:S(2)}, u32[]{:S(2)}) collective-permute-start(f32[1,32,1600]{2,1,0:T(8,128)S(1)} %get-tuple-element.1302), channel_id=1, source_target_pairs={{0,4},{4,8},{8,12},{1,5},{5,9},{9,13},{2,6},{6,10},{10,14},{3,7},{... | collective-permute-start | bytes 614408 | tf_op jit(solution)/shard_map/while/body/eval_jaxpr/ppermute | solution.py:15
  65.1 9.2 collective-permute-start
  86.4 8.3 collective-permute-start
  106.8 7.7 collective-permute-start
  116.2 18.1 %collective-permute-start = (f32[1,32,1600]{2,1,0:T(8,128)S(1)}, f32[1,32,1600]{2,1,0:T(8,128)S(1)}, u32[]{:S(2)}, u32[]{:S(2)}) collective-permute-start(f32[1,32,1600]{2,1,0:T(8,128)S(1)} %get-tuple-element.1302), channel_id=1, source_target_pairs={{0,4},{4,8},{8,12},{1,5},{5,9},{9,13},{2,6},{6,10},{10,14},{3,7},{... | collective-permute-start | bytes 614408 | tf_op jit(solution)/shard_map/while/body/eval_jaxpr/ppermute | solution.py:15
  136.1 7.7 collective-permute-start
  145.5 16.2 %collective-permute-start = (f32[1,32,1600]{2,1,0:T(8,128)S(1)}, f32[1,32,1600]{2,1,0:T(8,128)S(1)}, u32[]{:S(2)}, u32[]{:S(2)}) collective-permute-start(f32[1,32,1600]{2,1,0:T(8,128)S(1)} %get-tuple-element.1302), channel_id=1, source_target_pairs={{0,4},{4,8},{8,12},{1,5},{5,9},{9,13},{2,6},{6,10},{10,14},{3,7},{... | collective-permute-start | bytes 614408 | tf_op jit(solution)/shard_map/while/body/eval_jaxpr/ppermute | solution.py:15
  161.7 8.3 copy-start.18
  161.7 8.3 copy-start.20
  161.7 57.7 %copy-start.16 = (s32[4,1,384]{2,1,0:T(1,128)S(1)}, s32[4,1,384]{2,1,0:T(1,128)}, u32[]{:S(2)}) copy-start(s32[4,1,384]{2,1,0:T(1,128)} %param.23) | copy-start | bytes 18436
  161.7 57.7 %copy-start.17 = (s32[4,1,384]{2,1,0:T(1,128)S(1)}, s32[4,1,384]{2,1,0:T(1,128)}, u32[]{:S(2)}) copy-start(s32[4,1,384]{2,1,0:T(1,128)} %param.24) | copy-start | bytes 18436
  161.8 57.7 %copy-start.19 = (f32[4,1,384]{2,1,0:T(1,128)S(1)}, f32[4,1,384]{2,1,0:T(1,128)}, u32[]{:S(2)}) copy-start(f32[4,1,384]{2,1,0:T(1,128)} %param.25) | copy-start | bytes 18436
  170.0 134.6 %all-reduce.11.cloned.1.call-start = ((), (), s32[]{:S(2)}) async-start(), calls=%async_computation.8 | async-start | bytes 262144 | tf_op jit(solution)/shard_map/psum | solution.py:20
  226.0 450.6 %reduce-scatter.24.cloned.1.call-start = ((), (), s32[]{:S(2)}) async-start(), calls=%async_computation.13 | async-start | bytes 3584000
  318.8 6.8 collective-permute-start.1
  328.8 6.8 collective-permute-start.1
  338.9 93.1 %collective-permute-start.1 = (bf16[1,32,1600]{2,1,0:T(8,128)(2,1)}, bf16[1,32,1600]{2,1,0:T(8,128)(2,1)S(1)}, u32[]{:S(2)}, u32[]{:S(2)}) collective-permute-start(bf16[1,32,1600]{2,1,0:T(8,128)(2,1)} %get-tuple-element.1167), channel_id=1, source_target_pairs={{4,0},{8,4},{12,8},{5,1},{9,5},{13,9},{6,2},{10,6},{14,10},{7,3},{... | collective-permute-start | bytes 307208 | tf_op jit(solution)/shard_map/while/body/eval_jaxpr/ppermute | solution.py:15
  461.2 3.8 copy-start.7
  465.1 7.6 collective-permute-start.1
  505.9 7.6 collective-permute-start.1
  542.7 3.8 copy-start.7
  546.6 7.6 collective-permute-start.1
  587.3 7.0 collective-permute-start.1
  613.5 74.4 %reduce-scatter.26.cloned.1.call-start = ((), (), s32[]{:S(2)}) async-start(), calls=%async_computation.14 | async-start | bytes 3584000
  636.4 90.3 %reduce-scatter.22.cloned.1.call-start = ((), (), s32[]{:S(2)}) async-start(), calls=%async_computation.12 | async-start | bytes 3584000
  658.1 6.5 copy-start.11
  658.2 161.4 %reduce-scatter.18.cloned.1.call-start = ((), (), s32[]{:S(2)}) async-start(), calls=%async_computation.10 | async-start | bytes 7241728 | tf_op jit(solution)/shard_map/reduce_scatter | solution.py:301
  669.5 208.6 %reduce-scatter.28.cloned.1.call-start = ((), (), s32[]{:S(2)}) async-start(), calls=%async_computation.15 | async-start | bytes 139264
  671.2 265.4 %reduce-scatter.20.cloned.1.call-start = ((), (), s32[]{:S(2)}) async-start(), calls=%async_computation.11 | async-start | bytes 278528 | tf_op jit(solution)/shard_map/reduce_scatter | solution.py:304
  673.0 301.2 %reduce-scatter.16.cloned.1.call-start = ((), (), s32[]{:S(2)}) async-start(), calls=%async_computation.9 | async-start | bytes 3461120 | tf_op jit(solution)/shard_map/reduce_scatter | solution.py:296
  (35 other events, 96.7 us)
Sparse Core Ops, SparseCore 0:
  10.2 44.1 all-gather.1
  170.1 45.8 all-reduce.12
  226.1 78.4 all-reduce.10
  613.6 35.4 reduce-scatter.23
  651.7 36.2 reduce-scatter.25
  690.3 36.2 reduce-scatter.21
  731.1 88.3 reduce-scatter.17
  823.6 54.5 reduce-scatter.27
  882.2 54.3 reduce-scatter.19
  939.6 34.5 reduce-scatter.15
where the time goes:
time: 987 us; the launch traced here: 981 us
  waiting for transfers between devices  475 us (48%)
  matrix products  149 us (15%)
  local copies, waits for them, and re-layouts  142 us (14%)
  other arithmetic  88.3 us (9%)
  starting transfers between devices  56.4 us (6%)
  blocking collectives  49.4 us (5%)
  between operations  19.4 us (2%)
    ppermute x14, waiting for transfers between devices, passed_along(): return lax.ppermute(block, axis, route)  111 us
    unnamed x14, waiting for transfers between devices  102 us
    reduce_scatter x1, waiting for transfers between devices, on_device(): lax.psum_scatter(grad_reassemble.astype(jnp.float32), ('section', 'dp'),...  90.1 us
    unnamed x43, local copies, waits for them, and re-layouts  85.7 us
    psum x2, waiting for transfers between devices, broadcast(): return lax.psum(kept, axis)  75.9 us
    select_n x42, other arithmetic, put_slot(): return jnp.where(active, updated, store_array)  65.6 us
    reduce_scatter x1, waiting for transfers between devices, on_device(): lax.psum_scatter(grad_merging.astype(jnp.float32), ('section', 'dp'), sca...  58.5 us
    ppermute x14, starting transfers between devices, passed_along(): return lax.ppermute(block, axis, route)  55.6 us
  transfers between devices with their start and end apart: 24, of which 20 were waited for; matrix products, arithmetic and copies ran while one was open for 20% of the time, Pallas kernels for 0%

commit v1 on v0

--- a/solution.py
+++ b/solution.py
@@ -7,6 +7,7 @@
 HEADS = 13
 NHOOK = 4
 EPS = 1e-06
+deliver_series_on = lambda block_in, lane_axis: jnp.sum(lax.all_gather(block_in, lane_axis), 0)
 
 
 def passed_along(block, axis, distance):
@@ -17,7 +18,7 @@
 
 def broadcast(value, axis, source):
     kept = jnp.where(lax.axis_index(axis) == source, value, 0).astype(value.dtype)
-    return lax.psum(kept, axis)
+    return deliver_series_on(kept, axis)
 
 
 def as_sent(x):

time: 987 us -> 1030 us (1.044)
  blocking collectives: 49.4 us -> 175 us
  waiting for transfers between devices: 475 us -> 397 us
    all_gather x0 -> x5, blocking collectives: none -> 131 us  [lax.all_gather(block_in, lane_axis)]
    psum x2 -> x0, waiting for transfers between devices: 75.9 us -> none  [broadcast(): return lax.psum(kept, axis)]
    unnamed x14 -> x12, waiting for transfers between devices: 102 us -> 103 us
  transfers between devices with their start and end apart: 24 -> 22, of which waited for: 20 -> 19; matrix products, arithmetic and copies ran while one was open for 20% -> 19% of each run, Pallas kernels for 0% -> 0%
where the time goes in v1:
time: 1030 us
  waiting for transfers between devices  397 us (39%)
  blocking collectives  175 us (17%)
  matrix products  147 us (14%)
  local copies, waits for them, and re-layouts  143 us (14%)
  other arithmetic  87.6 us (9%)
  starting transfers between devices  56.1 us (5%)
  between operations  19.6 us (2%)
    all_gather x5, blocking collectives, lax.all_gather(block_in, lane_axis)  131 us
    ppermute x14, waiting for transfers between devices, passed_along(): return lax.ppermute(block, axis, route)  108 us
    unnamed x12, waiting for transfers between devices  103 us
    reduce_scatter x1, waiting for transfers between devices, on_device(): lax.psum_scatter(grad_reassemble.astype(jnp.float32), ('section', 'dp'),...  90.1 us
    unnamed x43, local copies, waits for them, and re-layouts  87.1 us
    select_n x42, other arithmetic, put_slot(): return jnp.where(active, updated, store_array)  65.6 us
    reduce_scatter x1, waiting for transfers between devices, on_device(): lax.psum_scatter(grad_merging.astype(jnp.float32), ('section', 'dp'), sca...  58.4 us
    ppermute x14, starting transfers between devices, passed_along(): return lax.ppermute(block, axis, route)  55.5 us
  transfers between devices with their start and end apart: 22, of which 19 were waited for; matrix products, arithmetic and copies ran while one was open for 19% of the time, Pallas kernels for 0%

profile of v1, /device:TPU:0, one launch (start us, length us, event | category | flops | bytes accessed | tf_op | source)
XLA Modules:
  0.0 1026.1 jit_solution(6272283539864168442)
XLA Ops:
  16.0 24.9 %all_gather.47 = bf16[128,196]{1,0:T(8,128)(2,1)} all-gather(bf16[8,196]{1,0:T(8,128)(2,1)} %param.33), channel_id=1, replica_groups=mesh['group'=2,'section'=4,'dp'=4] {'section','dp'}, dimensions={0}, use_global_device_ids=true | all-gather | bytes 53312 | tf_op jit(solution)/shard_map/all_gather | solution.py:139
  40.9 19.3 %all_gather.46 = bf16[4,128,128]{1,0,2:T(4,128)(2,1)} all-gather(bf16[4,128,8]{1,0,2:T(4,128)(2,1)S(1)} %copy.217), channel_id=1, replica_groups=mesh['group'=2,'section'=4,'dp'=4] {'section','dp'}, dimensions={2}, use_global_device_ids=true | all-gather | bytes 139264 | tf_op jit(solution)/shard_map/all_gather | solution.py:138
  66.2 5.3 copy.216
  71.5 5.3 copy.214
  77.8 126.7 %while.42 = (s32[]{:T(128)}, f32[1,32,1600]{2,1,0:T(8,128)S(1)}, f32[4,1,32,1600]{3,2,1,0:T(8,128)}, bf16[4,1,32,1600]{3,2,1,0:T(8,128)(2,1)}, s32[]{:T(128)}, /...) while((s32[]{:T(128)}, f32[1,32,1600]{2,1,0:T(8,128)S(1)}, ...), condition=%wide.region_6.7_spmd, body=%wide.region_0.6_spmd.sunk | while | flops 344828992 | bytes 25776712 | solution.py:165
  79.5 10.4 %conditional.7 = (f32[1,32,1600]{2,1,0:T(8,128)S(1)}) conditional(s32[]{:T(128)} %convert_element_type.825, f32[1,32,1600]{2,1,0:T(8,128)S(1)} %get-tuple-element.1180, (f32[1,32,1600]{2,1,0:T(8,128)S(1)}, bf16[1600,832]{1,0:T(8,128)(2,1)}, bf16[1600,832]{1,0:T(8,128)(2,1)S(1)}, bf16[1600,832]{1,0:T(8,128)(2,1)}, bf16[832,1600]{1,0:T(8,128)(2,1)}) %tuple.169), branch_computations={%region_1.1_spmd, %region_2.5_spmd} | conditional | flops 344624192 | bytes 23596836 | solution.py:159
  98.1 10.4 %conditional.7 = (f32[1,32,1600]{2,1,0:T(8,128)S(1)}) conditional(s32[]{:T(128)} %convert_element_type.825, f32[1,32,1600]{2,1,0:T(8,128)S(1)} %get-tuple-element.1180, (f32[1,32,1600]{2,1,0:T(8,128)S(1)}, bf16[1600,832]{1,0:T(8,128)(2,1)}, bf16[1600,832]{1,0:T(8,128)(2,1)S(1)}, bf16[1600,832]{1,0:T(8,128)(2,1)}, bf16[832,1600]{1,0:T(8,128)(2,1)}) %tuple.169), branch_computations={%region_1.1_spmd, %region_2.5_spmd} | conditional | flops 344624192 | bytes 23596836 | solution.py:159
  119.1 10.4 %conditional.7 = (f32[1,32,1600]{2,1,0:T(8,128)S(1)}) conditional(s32[]{:T(128)} %convert_element_type.825, f32[1,32,1600]{2,1,0:T(8,128)S(1)} %get-tuple-element.1180, (f32[1,32,1600]{2,1,0:T(8,128)S(1)}, bf16[1600,832]{1,0:T(8,128)(2,1)}, bf16[1600,832]{1,0:T(8,128)(2,1)S(1)}, bf16[1600,832]{1,0:T(8,128)(2,1)}, bf16[832,1600]{1,0:T(8,128)(2,1)}) %tuple.169), branch_computations={%region_1.1_spmd, %region_2.5_spmd} | conditional | flops 344624192 | bytes 23596836 | solution.py:159
  139.1 10.4 %conditional.7 = (f32[1,32,1600]{2,1,0:T(8,128)S(1)}) conditional(s32[]{:T(128)} %convert_element_type.825, f32[1,32,1600]{2,1,0:T(8,128)S(1)} %get-tuple-element.1180, (f32[1,32,1600]{2,1,0:T(8,128)S(1)}, bf16[1600,832]{1,0:T(8,128)(2,1)}, bf16[1600,832]{1,0:T(8,128)(2,1)S(1)}, bf16[1600,832]{1,0:T(8,128)(2,1)}, bf16[832,1600]{1,0:T(8,128)(2,1)}) %tuple.169), branch_computations={%region_1.1_spmd, %region_2.5_spmd} | conditional | flops 344624192 | bytes 23596836 | solution.py:159
  158.9 14.8 %collective-permute-start = (f32[1,32,1600]{2,1,0:T(8,128)S(1)}, f32[1,32,1600]{2,1,0:T(8,128)S(1)}, u32[]{:S(2)}, u32[]{:S(2)}) collective-permute-start(f32[1,32,1600]{2,1,0:T(8,128)S(1)} %get-tuple-element.1329), channel_id=1, source_target_pairs={{0,4},{4,8},{8,12},{1,5},{5,9},{9,13},{2,6},{6,10},{10,14},{3,7},{... | collective-permute-start | bytes 614408 | tf_op jit(solution)/shard_map/while/body/eval_jaxpr/ppermute | solution.py:16
  188.2 12.9 %collective-permute-start = (f32[1,32,1600]{2,1,0:T(8,128)S(1)}, f32[1,32,1600]{2,1,0:T(8,128)S(1)}, u32[]{:S(2)}, u32[]{:S(2)}) collective-permute-start(f32[1,32,1600]{2,1,0:T(8,128)S(1)} %get-tuple-element.1329), channel_id=1, source_target_pairs={{0,4},{4,8},{8,12},{1,5},{5,9},{9,13},{2,6},{6,10},{10,14},{3,7},{... | collective-permute-start | bytes 614408 | tf_op jit(solution)/shard_map/while/body/eval_jaxpr/ppermute | solution.py:16
  205.9 24.5 %all-gather = bf16[512,128]{1,0:T(8,128)(2,1)S(1)} all-gather(bf16[128,128]{1,0:T(8,128)(2,1)S(1)} %fusion.117), channel_id=2, replica_groups=mesh['group'=2,'section'=4,'dp'=4] {'section'}, dimensions={0}, use_global_device_ids=true | all-gather | bytes 163840 | tf_op jit(solution)/shard_map/all_gather | solution.py:10
  231.8 14.2 %all-gather.1 = bf16[512,128]{1,0:T(8,128)(2,1)} all-gather(bf16[128,128]{1,0:T(8,128)(2,1)S(1)} %fusion.118), channel_id=3, replica_groups=mesh['group'=2,'section'=4,'dp'=4] {'section'}, dimensions={0}, use_global_device_ids=true | all-gather | bytes 163840 | tf_op jit(solution)/shard_map/all_gather | solution.py:10
  247.4 14.2 %all-gather.2 = bf16[512,128]{1,0:T(8,128)(2,1)} all-gather(bf16[128,128]{1,0:T(8,128)(2,1)S(1)} %fusion.119), channel_id=4, replica_groups=mesh['group'=2,'section'=4,'dp'=4] {'section'}, dimensions={0}, use_global_device_ids=true | all-gather | bytes 163840 | tf_op jit(solution)/shard_map/all_gather | solution.py:10
  263.1 14.3 %all-gather.3 = bf16[512,128]{1,0:T(8,128)(2,1)} all-gather(bf16[128,128]{1,0:T(8,128)(2,1)S(1)} %fusion.120), channel_id=5, replica_groups=mesh['group'=2,'section'=4,'dp'=4] {'section'}, dimensions={0}, use_global_device_ids=true | all-gather | bytes 163840 | tf_op jit(solution)/shard_map/all_gather | solution.py:10
  277.3 4.9 conditional.3
  283.8 63.6 %all_gather.48 = bf16[4,4,128,128]{3,2,1,0:T(8,128)(2,1)S(1)} all-gather(bf16[1,4,128,128]{3,2,1,0:T(8,128)(2,1)S(1)} %maximum_select_fusion), channel_id=1, replica_groups=mesh['group'=2,'section'=4,'dp'=4] {'section'}, dimensions={0}, use_global_device_ids=true | all-gather | bytes 655360 | tf_op jit(solution)/shard_map/all_gather | solution.py:10
  358.6 280.3 %while.43 = (s32[]{:T(128)}, f32[1,32,1600]{2,1,0:T(8,128)S(1)}, bf16[4,3,32,832]{3,2,0,1:T(8,128)(2,1)}, bf16[4,32,1600]{2,1,0:T(8,128)(2,1)}, bf16[4,32,832]{2...) while((s32[]{:T(128)}, f32[1,32,1600]{2,1,0:T(8,128)S(1)}, ...), condition=%wide.region_24.25_spmd.clone, body=%wide.region_16.24_spmd.clone.sunk | while | flops 608857152 | bytes 61259056 | solution.py:273
  387.8 88.9 %collective-permute-done.1 = bf16[1,32,1600]{2,1,0:T(8,128)(2,1)S(1)} collective-permute-done((bf16[1,32,1600]{2,1,0:T(8,128)(2,1)}, bf16[1,32,1600]{2,1,0:T(8,128)(2,1)S(1)}, u32[]{:S(2)}, u32[]{:S(2)}) %collective-permute-start.1) | collective-permute-done | bytes 102432 | tf_op jit(solution)/shard_map/while/body/eval_jaxpr/ppermute | solution.py:16
  478.6 31.3 %conditional.8 = (bf16[1,32,1600]{2,1,0:T(8,128)(2,1)}, bf16[1,3,32,832]{3,2,1,0:T(8,128)(2,1)S(1)}, bf16[1,32,1600]{2,1,0:T(8,128)(2,1)}, bf16[1,32,832]{2,1,0:T(8,128)(2,1)S(1)}) conditional(s32[]{:T(128)} %convert_element_type.826, () %tuple.172, (f32[1,32,1600]{2,1,0:T(8,128)S(1)}, bf16[832,1600]{1,0:T(8,128)(2,1)}, ...), branch_computations={%region_17.17_spmd, %region_18.23_spmd} | conditional | flops 608443456 | bytes 57541052 | solution.py:252
  519.3 31.3 %conditional.8 = (bf16[1,32,1600]{2,1,0:T(8,128)(2,1)}, bf16[1,3,32,832]{3,2,1,0:T(8,128)(2,1)S(1)}, bf16[1,32,1600]{2,1,0:T(8,128)(2,1)}, bf16[1,32,832]{2,1,0:T(8,128)(2,1)S(1)}) conditional(s32[]{:T(128)} %convert_element_type.826, () %tuple.172, (f32[1,32,1600]{2,1,0:T(8,128)S(1)}, bf16[832,1600]{1,0:T(8,128)(2,1)}, ...), branch_computations={%region_17.17_spmd, %region_18.23_spmd} | conditional | flops 608443456 | bytes 57541052 | solution.py:252
  560.0 31.3 %conditional.8 = (bf16[1,32,1600]{2,1,0:T(8,128)(2,1)}, bf16[1,3,32,832]{3,2,1,0:T(8,128)(2,1)S(1)}, bf16[1,32,1600]{2,1,0:T(8,128)(2,1)}, bf16[1,32,832]{2,1,0:T(8,128)(2,1)S(1)}) conditional(s32[]{:T(128)} %convert_element_type.826, () %tuple.172, (f32[1,32,1600]{2,1,0:T(8,128)S(1)}, bf16[832,1600]{1,0:T(8,128)(2,1)}, ...), branch_computations={%region_17.17_spmd, %region_18.23_spmd} | conditional | flops 608443456 | bytes 57541052 | solution.py:252
  600.7 31.3 %conditional.8 = (bf16[1,32,1600]{2,1,0:T(8,128)(2,1)}, bf16[1,3,32,832]{3,2,1,0:T(8,128)(2,1)S(1)}, bf16[1,32,1600]{2,1,0:T(8,128)(2,1)}, bf16[1,32,832]{2,1,0:T(8,128)(2,1)S(1)}) conditional(s32[]{:T(128)} %convert_element_type.826, () %tuple.172, (f32[1,32,1600]{2,1,0:T(8,128)S(1)}, bf16[832,1600]{1,0:T(8,128)(2,1)}, ...), branch_computations={%region_17.17_spmd, %region_18.23_spmd} | conditional | flops 608443456 | bytes 57541052 | solution.py:252
  641.0 12.4 %copy.242 = bf16[1,1600,832]{2,0,1:T(2,128)(2,1)} copy(bf16[1,1600,832]{1,2,0:T(8,128)(2,1)S(1)} %fusion.92) | data formatting | bytes 5324800
  661.7 14.5 %copy.244 = bf16[1,1600,832]{2,0,1:T(2,128)(2,1)} copy(bf16[1,1600,832]{1,2,0:T(8,128)(2,1)} %fusion.93) | data formatting | bytes 5324800
  683.6 14.3 %copy.240 = bf16[1,1600,832]{2,0,1:T(2,128)(2,1)} copy(bf16[1,1600,832]{1,2,0:T(8,128)(2,1)} %fusion.91) | data formatting | bytes 5324800
  723.9 9.3 reduce-scatter.26.cloned.1.call-done
  736.0 35.9 %reduce-scatter.22.cloned.1.call-done = bf16[400,832]{1,0:T(8,128)(2,1)} async-done(((bf16[1600,832]{1,0:T(8,128)(2,1)}), bf16[400,832]{1,0:T(8,128)(2,1)}) %reduce-scatter.22.cloned.1.call-update) | async-done | bytes 665616
  774.7 90.1 %reduce-scatter.18.cloned.1.call-done = f32[5,1600,8]{1,0,2:T(8,128)} async-done(((f32[5,1600,128]{1,0,2:T(8,128)}), f32[5,1600,8]{1,0,2:T(8,128)}) %reduce-scatter.18.cloned.1.call-update) | async-done | bytes 256016 | tf_op jit(solution)/shard_map/reduce_scatter | solution.py:302
  866.5 56.6 %reduce-scatter.28.cloned.1.call-done = f32[8,196]{1,0:T(8,128)} async-done(((f32[128,196]{1,0:T(8,128)}), f32[8,196]{1,0:T(8,128)}) %reduce-scatter.28.cloned.1.call-update) | async-done | bytes 6288
  923.1 58.4 %reduce-scatter.20.cloned.1.call-done = f32[4,128,8]{1,2,0:T(8,128)} async-done(((f32[4,128,128]{1,2,0:T(8,128)}), f32[4,128,8]{1,2,0:T(8,128)}) %reduce-scatter.20.cloned.1.call-update) | async-done | bytes 16400 | tf_op jit(solution)/shard_map/reduce_scatter | solution.py:305
  981.5 37.8 %reduce-scatter.16.cloned.1.call-done = bf16[1,208,1600]{2,1,0:T(8,128)(2,1)} async-done(((bf16[1,832,1600]{2,1,0:T(8,128)(2,1)}), bf16[1,208,1600]{2,1,0:T(8,128)(2,1)}) %reduce-scatter.16.cloned.1.call-update) | async-done | bytes 665616 | tf_op jit(solution)/shard_map/reduce_scatter | solution.py:297
  (456 shorter events, 377.7 us)
Async XLA Ops:
  7.2 197.3 %all-gather.6.cloned.1.call-start = ((), (), s32[]{:S(2)}) async-start(), calls=%async_computation.7 | async-start | bytes 2263040 | tf_op jit(solution)/shard_map/all_gather | solution.py:137
  7.9 713.1 %reduce-scatter.24.cloned.1.call-start = ((), (), s32[]{:S(2)}) async-start(), calls=%async_computation.12 | async-start | bytes 3584000
  89.9 6.6 collective-permute-start
  108.5 8.8 collective-permute-start
  129.4 7.9 collective-permute-start
  149.5 7.7 collective-permute-start
  158.9 18.1 %collective-permute-start = (f32[1,32,1600]{2,1,0:T(8,128)S(1)}, f32[1,32,1600]{2,1,0:T(8,128)S(1)}, u32[]{:S(2)}, u32[]{:S(2)}) collective-permute-start(f32[1,32,1600]{2,1,0:T(8,128)S(1)} %get-tuple-element.1329), channel_id=1, source_target_pairs={{0,4},{4,8},{8,12},{1,5},{5,9},{9,13},{2,6},{6,10},{10,14},{3,7},{... | collective-permute-start | bytes 614408 | tf_op jit(solution)/shard_map/while/body/eval_jaxpr/ppermute | solution.py:16
  178.8 7.7 collective-permute-start
  188.2 16.2 %collective-permute-start = (f32[1,32,1600]{2,1,0:T(8,128)S(1)}, f32[1,32,1600]{2,1,0:T(8,128)S(1)}, u32[]{:S(2)}, u32[]{:S(2)}) collective-permute-start(f32[1,32,1600]{2,1,0:T(8,128)S(1)} %get-tuple-element.1329), channel_id=1, source_target_pairs={{0,4},{4,8},{8,12},{1,5},{5,9},{9,13},{2,6},{6,10},{10,14},{3,7},{... | collective-permute-start | bytes 614408 | tf_op jit(solution)/shard_map/while/body/eval_jaxpr/ppermute | solution.py:16
  204.4 72.9 %copy-start.15 = (bf16[128,196]{1,0:T(8,128)(2,1)S(1)}, bf16[128,196]{1,0:T(8,128)(2,1)}, u32[]{:S(2)}) copy-start(bf16[128,196]{1,0:T(8,128)(2,1)} %all_gather.47) | copy-start | bytes 150532
  204.4 72.9 %copy-start.18 = (s32[4,1,384]{2,1,0:T(1,128)S(1)}, s32[4,1,384]{2,1,0:T(1,128)}, u32[]{:S(2)}) copy-start(s32[4,1,384]{2,1,0:T(1,128)} %param.23) | copy-start | bytes 18436
  204.4 72.9 %copy-start.19 = (s32[4,1,384]{2,1,0:T(1,128)S(1)}, s32[4,1,384]{2,1,0:T(1,128)}, u32[]{:S(2)}) copy-start(s32[4,1,384]{2,1,0:T(1,128)} %param.24) | copy-start | bytes 18436
  204.4 72.9 %copy-start.20 = (f32[4,1,384]{2,1,0:T(1,128)S(1)}, f32[4,1,384]{2,1,0:T(1,128)}, u32[]{:S(2)}) copy-start(f32[4,1,384]{2,1,0:T(1,128)} %param.25) | copy-start | bytes 18436
  347.5 6.4 copy-start.13
  351.5 7.1 copy-start.9
  361.8 6.8 collective-permute-start.1
  371.8 6.8 collective-permute-start.1
  381.8 94.9 %collective-permute-start.1 = (bf16[1,32,1600]{2,1,0:T(8,128)(2,1)}, bf16[1,32,1600]{2,1,0:T(8,128)(2,1)S(1)}, u32[]{:S(2)}, u32[]{:S(2)}) collective-permute-start(bf16[1,32,1600]{2,1,0:T(8,128)(2,1)} %get-tuple-element.1198), channel_id=1, source_target_pairs={{4,0},{8,4},{12,8},{5,1},{9,5},{13,9},{6,2},{10,6},{14,10},{7,3},{... | collective-permute-start | bytes 307208 | tf_op jit(solution)/shard_map/while/body/eval_jaxpr/ppermute | solution.py:16
  506.0 3.8 copy-start.7
  509.8 7.6 collective-permute-start.1
  550.5 7.6 collective-permute-start.1
  587.4 3.8 copy-start.7
  591.2 7.6 collective-permute-start.1
  628.1 3.8 copy-start.7
  631.9 7.0 collective-permute-start.1
  658.1 75.1 %reduce-scatter.26.cloned.1.call-start = ((), (), s32[]{:S(2)}) async-start(), calls=%async_computation.13 | async-start | bytes 3584000
  680.8 91.0 %reduce-scatter.22.cloned.1.call-start = ((), (), s32[]{:S(2)}) async-start(), calls=%async_computation.11 | async-start | bytes 3584000
  702.6 6.4 copy-start.12
  702.6 162.1 %reduce-scatter.18.cloned.1.call-start = ((), (), s32[]{:S(2)}) async-start(), calls=%async_computation.9 | async-start | bytes 7241728 | tf_op jit(solution)/shard_map/reduce_scatter | solution.py:302
  713.9 209.2 %reduce-scatter.28.cloned.1.call-start = ((), (), s32[]{:S(2)}) async-start(), calls=%async_computation.14 | async-start | bytes 139264
  715.7 265.8 %reduce-scatter.20.cloned.1.call-start = ((), (), s32[]{:S(2)}) async-start(), calls=%async_computation.10 | async-start | bytes 278528 | tf_op jit(solution)/shard_map/reduce_scatter | solution.py:305
  717.5 301.8 %reduce-scatter.16.cloned.1.call-start = ((), (), s32[]{:S(2)}) async-start(), calls=%async_computation.8 | async-start | bytes 3461120 | tf_op jit(solution)/shard_map/reduce_scatter | solution.py:297
  (33 other events, 87.2 us)
Sparse Core Ops, SparseCore 0:
  10.2 44.4 all-gather.5
  658.2 35.9 reduce-scatter.23
  696.9 36.2 reduce-scatter.25
  735.6 36.2 reduce-scatter.21
  776.2 88.4 reduce-scatter.17
  868.6 54.4 reduce-scatter.27
  927.2 54.2 reduce-scatter.19
  984.6 34.5 reduce-scatter.15
